TPU v7x, 256 devices: a whole 4x4x8 slice. The times are simulated.
256 devices in a mesh: wide: 32 (over y, x, core), narrow: 8 (over z).
Axes of the slice: x: 4, y: 4, z: 8, core: 2. Of those that a mesh axis runs over, the one named last changes fastest.
Arguments:
- noise: float32 [1024, 1024, 128], P('narrow', 'wide'), may hold values from -6 to 6
- spectrum: float32 [128, 1024, 1024], P('wide', None, 'narrow'), may hold values from 0.1 to 8.5, as said below
- assay: bfloat16 [256, 512], P(('wide', 'narrow')), may hold values from -5 to 5
- measure_weights: bfloat16 [256, 512, 4, 128], P(('wide', 'narrow')), may hold values from -3 to 3
- measure_owner: int32 [256, 512], P(('wide', 'narrow')), may hold values from 0 to 255, as said below
- measure_cell: int32 [256, 512], P(('wide', 'narrow')), may hold values from 0 to 524287
- measure_pencils: int32 [256, 512, 4], P(('wide', 'narrow')), may hold values from 0 to 4095
Outputs:
- conditioned: float32 [1024, 1024, 128], P('narrow', 'wide')
Inputs may be any that keep to these rules, and one draw needn't show every extreme that they name: `spectrum`: Positive, with rough factors from frequency to frequency. `measure_owner`: devices are numbered with narrow fastest. At most 8 measurements of one device share an owner; one owner, drawn from the seed, receives exactly 8 from every device. `measure_cell`: cells of the owner's block are numbered with z fastest, then y, then x. `measure_pencils`: pencils of the owner's block are numbered with y fastest.
All inputs are finite; a program needn't handle non-finite values.
Results may differ from a plain program's by a relative error of at most 0.0003.
Values may be sent and summed in bfloat16 or wider, within the bound.
A program may use at most 128 MiB of HBM per device.

v0:
```python
import math
import jax
import jax.numpy as jnp
from jax import lax
from jax.sharding import PartitionSpec as P

CELLS_FIRST = 1024
CELLS_SECOND = 1024
CELLS_THIRD = 128
TARGET_PENCILS = 4
highest = lax.Precision.HIGHEST


def pair_tables(cosine, sine):
    upper = jnp.stack([cosine, sine], axis=1)
    lower = jnp.stack([-sine, cosine], axis=1)
    return jnp.stack([upper, lower])


def dft_matrix(length, sign):
    index = jnp.arange(length, dtype=jnp.int32)
    phase = index[:, None] * index[None, :] % length
    angle = phase.astype(jnp.float32) * (2.0 * math.pi / length)
    return pair_tables(jnp.cos(angle), sign * jnp.sin(angle))


def slot_depth(depth, half):
    slots = jnp.arange(depth, dtype=jnp.int32)
    span = 2 * half
    base = slots // span * half + slots % span % half
    mirror = jnp.where(base > 0, depth - base, depth // 2)
    return jnp.where(slots % span < half, base, mirror)


def arranged_tables(depth, half, sign):
    depth_of = slot_depth(depth, half)
    cell_list = jnp.arange(depth, dtype=jnp.int32)
    phase = depth_of[:, None] * cell_list[None, :] % depth
    angle = phase.astype(jnp.float32) * (2.0 * math.pi / depth)
    return (jnp.cos(angle), sign * jnp.sin(angle))


def transform(block, sign):
    outer = block.shape[1]
    length = block.shape[2]
    inner = block.shape[3]
    rows_q = 128
    rows_p = length // rows_q
    four = block.reshape(2, outer, rows_p, rows_q, inner)
    four = jnp.einsum("sapqb,sptc->tacqb", four, dft_matrix(rows_p, sign), precision=highest)
    index_p = jnp.arange(rows_p, dtype=jnp.int32)
    index_q = jnp.arange(rows_q, dtype=jnp.int32)
    angle = (index_p[:, None] * index_q[None, :] % length).astype(jnp.float32) * (
        2.0 * math.pi / length
    )
    twist_cos = jnp.cos(angle)[None, :, :, None]
    twist_sin = (sign * jnp.sin(angle))[None, :, :, None]
    four = jnp.stack(
        [four[0] * twist_cos - four[1] * twist_sin, four[0] * twist_sin + four[1] * twist_cos]
    )
    four = jnp.einsum("sacqb,sqtd->tadcb", four, dft_matrix(rows_q, sign), precision=highest)
    return four.reshape(2, outer, length, inner)


def rows_then_turn(block):
    return jnp.swapaxes(transform(block, -1.0), 2, 3)


def forward_along(block):
    return transform(block, -1.0)


def turn_then_rows(block):
    return transform(jnp.swapaxes(block, 2, 3), 1.0)


def local(noise, spectrum, assay, measure_weights, measure_owner, measure_cell, measure_pencils):
    size_x, size_y, depth = noise.shape
    half = spectrum.shape[0] // 2
    tables = jnp.stack(arranged_tables(depth, half, -1.0))
    spectral = jnp.einsum("xyz,sqz->sqyx", noise, tables, precision=highest)
    spectral = rows_then_turn(
        lax.all_to_all(spectral, "wide", split_axis=1, concat_axis=2, tiled=True)
    )
    spectral = forward_along(
        lax.all_to_all(spectral, "narrow", split_axis=3, concat_axis=2, tiled=True)
    )
    scaled = spectrum * (1.0 / (CELLS_FIRST * CELLS_SECOND * CELLS_THIRD))
    spectral = transform(spectral * scaled[None], 1.0)
    spectral = turn_then_rows(
        lax.all_to_all(spectral, "narrow", split_axis=2, concat_axis=3, tiled=True)
    )
    cos_rows, sin_rows = arranged_tables(depth, half, 1.0)
    inverse_tables = jnp.stack([cos_rows, -sin_rows])
    field = jnp.einsum(
        "sqyx,sqz->xyz",
        lax.all_to_all(spectral, "wide", split_axis=2, concat_axis=1, tiled=True),
        inverse_tables,
        precision=highest,
    )
    n_wide = lax.axis_size("wide")
    n_narrow = lax.axis_size("narrow")
    owner_device = measure_owner.reshape(-1)
    count = owner_device.shape[0]
    capacity = max(4, 4 * count // (n_wide * n_narrow))
    row_index = jnp.arange(count, dtype=jnp.int32)
    earlier = row_index[None, :] < row_index[:, None]
    same_owner = owner_device[None, :] == owner_device[:, None]
    slot_position = jnp.sum(same_owner & earlier, axis=1, dtype=jnp.int32)
    wide_target = owner_device // n_narrow
    narrow_target = owner_device % n_narrow
    weight_holder = jnp.zeros((n_wide, n_narrow, capacity, TARGET_PENCILS, depth), jnp.bfloat16)
    weight_holder = weight_holder.at[wide_target, narrow_target, slot_position].set(
        measure_weights[0]
    )
    assay_buf = jnp.zeros((n_wide, n_narrow, capacity), jnp.bfloat16)
    assay_buf = assay_buf.at[wide_target, narrow_target, slot_position].set(assay[0])
    row_indices = jnp.concatenate([measure_cell[0][:, None], measure_pencils[0]], axis=1)
    index_buf = jnp.zeros((n_wide, n_narrow, capacity, TARGET_PENCILS + 1), jnp.int32)
    index_buf = index_buf.at[wide_target, narrow_target, slot_position].set(row_indices)
    weight_got, assay_got, index_got = (
        lax.all_to_all(
            lax.all_to_all(weight_holder, "wide", split_axis=0, concat_axis=0, tiled=True),
            "narrow",
            split_axis=1,
            concat_axis=1,
            tiled=True,
        ),
        lax.all_to_all(
            lax.all_to_all(assay_buf, "wide", split_axis=0, concat_axis=0, tiled=True),
            "narrow",
            split_axis=1,
            concat_axis=1,
            tiled=True,
        ),
        lax.all_to_all(
            lax.all_to_all(index_buf, "wide", split_axis=0, concat_axis=0, tiled=True),
            "narrow",
            split_axis=1,
            concat_axis=1,
            tiled=True,
        ),
    )
    index_got = index_got.reshape(-1, TARGET_PENCILS + 1)
    cell_list = index_got[:, 0]
    targets = index_got[:, 1:].reshape(-1)
    value = field.reshape(-1)[cell_list]
    resid = assay_got.reshape(-1).astype(jnp.float32) - value
    contrib = resid[:, None, None] * weight_got.reshape(-1, TARGET_PENCILS, depth).astype(
        jnp.float32
    )
    correction = (
        jnp.zeros((size_x * size_y, depth), jnp.float32).at[targets].add(contrib.reshape(-1, depth))
    )
    return field + correction.reshape(size_x, size_y, depth)


def solution(mesh):
    placed = (
        P("narrow", "wide", None),
        P("wide", None, "narrow"),
        P(("wide", "narrow"), None),
        P(("wide", "narrow"), None, None, None),
        P(("wide", "narrow"), None),
        P(("wide", "narrow"), None),
        P(("wide", "narrow"), None, None),
    )
    return jax.shard_map(
        local, mesh=mesh, in_specs=placed, out_specs=P("narrow", "wide", None), check_vma=False
    )
```

profile of v0, /device:TPU:16, one launch (start us, length us, event | category | flops | bytes accessed | tf_op | source)
XLA Modules:
  0.0 602.8 jit_solution(5593420963950159069)
XLA Ops:
  1.6 6.0 %convolution_bitcast_fusion = f32[2,128,32,128]{3,1,2,0:T(8,128)S(1)} fusion(f32[128,32,128]{2,1,0:T(8,128)} %param.7, f32[1,128,128]{2,1,0:T(8,128)S(1)} %get-tuple-element.23, f32[1,128,128]{2,1,0:T(8,128)S(1)} %get-tuple-element.22), kind=kOutput, calls=%fused_computation.45 | convolution fusion | flops 1610645504 | bytes 6422528 | tf_op jit(solution)/shard_map/xyz,sqz->sqyx/dot_general | solution.py:81
  7.7 4.4 copy.272
  12.1 8.3 %all-to-all-start = ((f32[2,128,32,128]{3,2,0,1:T(8,128)}), f32[2,128,32,128]{3,2,0,1:T(8,128)}, u32[]{:S(2)}, u32[]{:S(2)}) async-start(f32[2,128,32,128]{3,2,0,1:T(8,128)} %copy.272), calls=%async_computation | async-start | bytes 8388608 | tf_op jit(solution)/shard_map/all_to_all | solution.py:83
  21.7 28.0 %scatter_fusion = s32[32,8,8,5]{3,2,1,0:T(8,128)S(1)} fusion(s32[32,8,8,5]{3,2,1,0:T(8,128)S(1)} %broadcast_in_dim.15, s32[512]{0:T(512)S(1)} %bitcast.210, s32[512,5]{1,0:T(8,128)S(1)} %copy.300), kind=kCustom, calls=%fused_computation.1 | custom fusion | bytes 36864 | tf_op jit(solution)/shard_map/scatter | solution.py:120
  52.5 29.6 %scatter_fusion.1 = bf16[32,8,8]{0,2,1:T(8,128)(2,1)S(1)} fusion(bf16[32,8,8]{0,2,1:T(8,128)(2,1)S(1)} %broadcast_in_dim.16, s32[512]{0:T(512)S(1)} %bitcast.211, bf16[512]{0:T(512)(128)(2,1)S(1)} %reduce), kind=kCustom, calls=%fused_computation.2 | custom fusion | bytes 9216 | tf_op jit(solution)/shard_map/scatter | solution.py:117
  83.7 7.3 %all-to-all-start.6 = ((bf16[32,8,8]{2,1,0:T(8,128)(2,1)}), bf16[32,8,8]{2,1,0:T(8,128)(2,1)S(1)}, u32[]{:S(2)}, u32[]{:S(2)}) async-start(bf16[32,8,8]{2,1,0:T(8,128)(2,1)} %copy.305), calls=%async_computation.6 | async-start | bytes 131072 | tf_op jit(solution)/shard_map/all_to_all | solution.py:130
  93.8 5.6 fusion.24
  102.2 7.6 %all-to-all-start.4 = ((s32[32,1,320]{2,1,0:T(1,128)}), s32[32,1,320]{2,1,0:T(1,128)S(1)}, u32[]{:S(2)}, u32[]{:S(2)}) async-start(s32[32,1,320]{2,1,0:T(1,128)} %reshape.696), calls=%async_computation.4 | async-start | bytes 98304 | tf_op jit(solution)/shard_map/all_to_all | solution.py:137
  109.8 6.6 %fusion.27 = f32[2,4,128,8,128]{4,2,3,1,0:T(8,128)S(1)} fusion(f32[2,4,8,128,128]{4,2,3,1,0:T(8,128)} %pad_maximum_fusion, f32[1,128,2,128]{1,3,0,2:T(8,128)S(1)} %get-tuple-element.14, f32[1,128,2,128]{1,3,0,2:T(8,128)S(1)} %get-tuple-element.15), kind=kOutput, calls=%fused_computation.38 | convolution fusion | flops 3221291008 | bytes 8650752 | tf_op jit(solution)/shard_map/sacqb,sqtd->tadcb/dot_general | solution.py:61
  118.8 4.7 copy.280
  123.5 8.6 %all-to-all-start.1 = ((f32[2,4,128,1024]{2,1,0,3:T(4,128)}), f32[2,4,128,1024]{2,1,0,3:T(4,128)}, u32[]{:S(2)}, u32[]{:S(2)}) async-start(f32[2,4,128,1024]{2,1,0,3:T(4,128)} %copy.280), calls=%async_computation.1 | async-start | bytes 8388608 | tf_op jit(solution)/shard_map/all_to_all | solution.py:86
  135.3 57.9 %scatter_fusion.2 = bf16[32,8,8,4,128]{4,3,2,1,0:T(4,128)(2,1)} fusion(bf16[32,8,8,4,128]{4,3,2,1,0:T(4,128)(2,1)} %broadcast_in_dim.17, s32[512]{0:T(512)S(1)} %bitcast.212, bf16[512,4,128]{2,1,0:T(4,128)(2,1)S(1)} %bitcast.229), kind=kCustom, calls=%fused_computation.3 | custom fusion | bytes 1579008 | tf_op jit(solution)/shard_map/scatter | solution.py:113
  198.3 30.5 %all-to-all-done.1 = f32[2,4,128,1024]{2,1,0,3:T(4,128)} async-done(((f32[2,4,128,1024]{2,1,0,3:T(4,128)}), f32[2,4,128,1024]{2,1,0,3:T(4,128)}, u32[]{:S(2)}, u32[]{:S(2)}) %all-to-all-start.1) | async-done | bytes 4194336 | tf_op jit(solution)/shard_map/all_to_all | solution.py:86
  232.2 4.2 copy.336
  236.4 7.8 %fusion.45 = f32[2,4,8,128,128]{4,2,3,1,0:T(8,128)} fusion(f32[2,4,128,8,128]{4,3,0,2,1:T(8,128)} %copy.336, f32[1,8,2,8]{1,3,0,2:T(8,128)S(1)} %copy.270, f32[1,8,2,8]{1,3,0,2:T(8,128)S(1)} %copy.269), kind=kOutput, calls=%fused_computation.44 | convolution fusion | flops 201326848 | bytes 8389632 | tf_op jit(solution)/shard_map/sapqb,sptc->tacqb/dot_general | solution.py:50
  244.2 7.1 %all-to-all-start.5 = ((s32[8,1,1280]{2,1,0:T(1,128)}), s32[8,1,1280]{2,1,0:T(1,128)S(1)}, u32[]{:S(2)}, u32[]{:S(2)}) async-start(s32[8,1,1280]{2,1,0:T(1,128)} %reshape.698), calls=%async_computation.5 | async-start | bytes 81920 | tf_op jit(solution)/shard_map/all_to_all | solution.py:136
  251.4 4.8 multiply_subtract_fusion.2
  259.5 7.8 %all-to-all-start.8 = ((bf16[32,8,8,4,128]{4,3,2,1,0:T(4,128)(2,1)}), bf16[32,8,8,4,128]{4,3,2,1,0:T(4,128)(2,1)}, u32[]{:S(2)}, u32[]{:S(2)}) async-start(bf16[32,8,8,4,128]{4,3,2,1,0:T(4,128)(2,1)} %scatter_fusion.2), calls=%async_computation.8 | async-start | bytes 4194304 | tf_op jit(solution)/shard_map/all_to_all | solution.py:123
  277.2 5.8 fusion.33
  283.8 4.1 fusion.36
  290.4 4.7 copy.289
  295.1 5.0 all-to-all-start.2
  303.8 93.1 %all-to-all-done.2 = f32[2,4,1024,128]{3,1,0,2:T(4,128)} async-done(((f32[2,4,1024,128]{3,1,0,2:T(4,128)}), f32[2,4,1024,128]{3,1,0,2:T(4,128)}, u32[]{:S(2)}, u32[]{:S(2)}) %all-to-all-start.2) | async-done | bytes 4194336 | tf_op jit(solution)/shard_map/all_to_all | solution.py:91
  400.5 5.0 copy.290
  405.5 5.4 copy.292
  411.0 5.4 fusion.39
  423.8 4.7 copy.296
  428.4 21.6 %all-to-all-done.9 = bf16[32,8,8,4,128]{4,3,2,0,1:T(4,128)(2,1)S(1)} async-done(((bf16[32,8,8,4,128]{4,3,2,0,1:T(4,128)(2,1)}), bf16[32,8,8,4,128]{4,3,2,0,1:T(4,128)(2,1)S(1)}, u32[]{:S(2)}, u32[]{:S(2)}) %all-to-all-start.9) | async-done | bytes 2097184 | tf_op jit(solution)/shard_map/all_to_all | solution.py:122
  450.0 7.8 %all-to-all-start.3 = ((f32[2,4,1024,128]{3,1,0,2:T(4,128)}), f32[2,4,1024,128]{3,1,0,2:T(4,128)}, u32[]{:S(2)}, u32[]{:S(2)}) async-start(f32[2,4,1024,128]{3,1,0,2:T(4,128)} %copy.296), calls=%async_computation.3 | async-start | bytes 8388608 | tf_op jit(solution)/shard_map/all_to_all | solution.py:97
  464.7 44.2 %all-to-all-done.3 = f32[2,4,1024,128]{3,1,0,2:T(4,128)} async-done(((f32[2,4,1024,128]{3,1,0,2:T(4,128)}), f32[2,4,1024,128]{3,1,0,2:T(4,128)}, u32[]{:S(2)}, u32[]{:S(2)}) %all-to-all-start.3) | async-done | bytes 4194336 | tf_op jit(solution)/shard_map/all_to_all | solution.py:97
  520.7 11.8 %gather_fusion = f32[2048]{0:T(1024)S(1)} fusion(f32[524288]{0:T(1024)S(1)} %bitcast.213, s32[2048]{0:T(1024)S(1)} %broadcast_clamp_fusion), kind=kCustom, calls=%fused_computation | custom fusion | bytes 24576 | tf_op jit(solution)/shard_map/gather | solution.py:147
  533.5 59.9 %scatter_custom_fusion.3 = f32[4096,128]{1,0:T(8,128)} fusion(s32[8192]{0:T(1024)S(1)} %bitcast.232, f32[8192,128]{1,0:T(8,128)} %bitcast.214, f32[8192]{0:T(1024)S(1)} %mul.834, f32[]{:T(128)} %constant.178.clone.1), kind=kCustom, calls=%fused_computation.35 | custom fusion | flops 2097152 | bytes 6324228 | tf_op jit(solution)/shard_map/scatter-add | solution.py:153
  (112 shorter events, 86.5 us)
Async XLA Ops:
  1.0 0.6 copy-start.1
  12.1 9.0 %copy-start.9 = (s32[1,512,4]{1,2,0:T(4,128)S(1)}, s32[1,512,4]{1,2,0:T(4,128)}, u32[]{:S(2)}) copy-start(s32[1,512,4]{1,2,0:T(4,128)} %param.13) | copy-start | bytes 24580
  12.1 9.0 %copy-start.11 = (s32[1,512]{1,0:T(1,128)S(1)}, s32[1,512]{1,0:T(1,128)}, u32[]{:S(2)}) copy-start(s32[1,512]{1,0:T(1,128)} %param.12) | copy-start | bytes 6148
  12.1 9.2 %copy-start.8 = (s32[1,512]{1,0:T(1,128)S(1)}, s32[1,512]{1,0:T(1,128)}, u32[]{:S(2)}) copy-start(s32[1,512]{1,0:T(1,128)} %param.11) | copy-start | bytes 6148
  12.1 71.6 %all-to-all-start = ((f32[2,128,32,128]{3,2,0,1:T(8,128)}), f32[2,128,32,128]{3,2,0,1:T(8,128)}, u32[]{:S(2)}, u32[]{:S(2)}) async-start(f32[2,128,32,128]{3,2,0,1:T(8,128)} %copy.272), calls=%async_computation | async-start | bytes 8388608 | tf_op jit(solution)/shard_map/all_to_all | solution.py:83
  21.1 78.4 %copy-start.3 = (f32[8,128]{0,1:T(8,128)}, f32[8,128]{0,1:T(8,128)S(1)}, u32[]{:S(2)}) copy-start(f32[8,128]{0,1:T(8,128)S(1)} %copy.277) | copy-start | bytes 12292
  21.1 31.3 %copy-start.10 = (bf16[1,512]{1,0:T(2,128)(2,1)S(1)}, bf16[1,512]{1,0:T(2,128)(2,1)}, u32[]{:S(2)}) copy-start(bf16[1,512]{1,0:T(2,128)(2,1)} %param.9) | copy-start | bytes 3076
  83.7 18.6 %all-to-all-start.6 = ((bf16[32,8,8]{2,1,0:T(8,128)(2,1)}), bf16[32,8,8]{2,1,0:T(8,128)(2,1)S(1)}, u32[]{:S(2)}, u32[]{:S(2)}) async-start(bf16[32,8,8]{2,1,0:T(8,128)(2,1)} %copy.305), calls=%async_computation.6 | async-start | bytes 131072 | tf_op jit(solution)/shard_map/all_to_all | solution.py:130
  102.2 21.2 %all-to-all-start.4 = ((s32[32,1,320]{2,1,0:T(1,128)}), s32[32,1,320]{2,1,0:T(1,128)S(1)}, u32[]{:S(2)}, u32[]{:S(2)}) async-start(s32[32,1,320]{2,1,0:T(1,128)} %reshape.696), calls=%async_computation.4 | async-start | bytes 98304 | tf_op jit(solution)/shard_map/all_to_all | solution.py:137
  123.5 11.8 %copy-start.6 = (bf16[1,512,4,128]{3,2,1,0:T(4,128)(2,1)S(1)}, bf16[1,512,4,128]{3,2,1,0:T(4,128)(2,1)}, u32[]{:S(2)}) copy-start(bf16[1,512,4,128]{3,2,1,0:T(4,128)(2,1)} %param.10) | copy-start | bytes 1572868
  123.5 105.4 %all-to-all-start.1 = ((f32[2,4,128,1024]{2,1,0,3:T(4,128)}), f32[2,4,128,1024]{2,1,0,3:T(4,128)}, u32[]{:S(2)}, u32[]{:S(2)}) async-start(f32[2,4,128,1024]{2,1,0,3:T(4,128)} %copy.280), calls=%async_computation.1 | async-start | bytes 8388608 | tf_op jit(solution)/shard_map/all_to_all | solution.py:86
  228.8 15.4 %all-to-all-start.7 = ((bf16[8,2,128]{2,1,0:T(2,128)(2,1)}), bf16[8,2,128]{2,1,0:T(2,128)(2,1)S(1)}, u32[]{:S(2)}, u32[]{:S(2)}) async-start(bf16[8,2,128]{2,1,0:T(2,128)(2,1)} %reshape.694), calls=%async_computation.7 | async-start | bytes 8192 | tf_op jit(solution)/shard_map/all_to_all | solution.py:129
  236.4 15.0 %copy-start.4 = (f32[8,128]{0,1:T(8,128)S(1)}, f32[8,128]{0,1:T(8,128)}, u32[]{:S(2)}) copy-start(f32[8,128]{0,1:T(8,128)} %copy-done.3) | copy-start | bytes 12292
  244.2 15.2 %all-to-all-start.5 = ((s32[8,1,1280]{2,1,0:T(1,128)}), s32[8,1,1280]{2,1,0:T(1,128)S(1)}, u32[]{:S(2)}, u32[]{:S(2)}) async-start(s32[8,1,1280]{2,1,0:T(1,128)} %reshape.698), calls=%async_computation.5 | async-start | bytes 81920 | tf_op jit(solution)/shard_map/all_to_all | solution.py:136
  259.5 35.6 %all-to-all-start.8 = ((bf16[32,8,8,4,128]{4,3,2,1,0:T(4,128)(2,1)}), bf16[32,8,8,4,128]{4,3,2,1,0:T(4,128)(2,1)}, u32[]{:S(2)}, u32[]{:S(2)}) async-start(bf16[32,8,8,4,128]{4,3,2,1,0:T(4,128)(2,1)} %scatter_fusion.2), calls=%async_computation.8 | async-start | bytes 4194304 | tf_op jit(solution)/shard_map/all_to_all | solution.py:123
  277.2 5.8 copy-start.5
  295.1 101.8 %all-to-all-start.2 = ((f32[2,4,1024,128]{3,1,0,2:T(4,128)}), f32[2,4,1024,128]{3,1,0,2:T(4,128)}, u32[]{:S(2)}, u32[]{:S(2)}) async-start(f32[2,4,1024,128]{3,1,0,2:T(4,128)} %copy.289), calls=%async_computation.2 | async-start | bytes 8388608 | tf_op jit(solution)/shard_map/all_to_all | solution.py:91
  396.9 53.1 %all-to-all-start.9 = ((bf16[32,8,8,4,128]{4,3,2,0,1:T(4,128)(2,1)}), bf16[32,8,8,4,128]{4,3,2,0,1:T(4,128)(2,1)S(1)}, u32[]{:S(2)}, u32[]{:S(2)}) async-start(bf16[32,8,8,4,128]{4,3,2,0,1:T(4,128)(2,1)} %copy.309), calls=%async_computation.9 | async-start | bytes 4194304 | tf_op jit(solution)/shard_map/all_to_all | solution.py:122
  450.0 58.9 %all-to-all-start.3 = ((f32[2,4,1024,128]{3,1,0,2:T(4,128)}), f32[2,4,1024,128]{3,1,0,2:T(4,128)}, u32[]{:S(2)}, u32[]{:S(2)}) async-start(f32[2,4,1024,128]{3,1,0,2:T(4,128)} %copy.296), calls=%async_computation.3 | async-start | bytes 8388608 | tf_op jit(solution)/shard_map/all_to_all | solution.py:97
  511.9 2.7 copy-start.2
  512.0 2.7 copy-start.7
  533.5 62.9 %copy-start = (f32[128,32,128]{0,2,1:T(8,128)S(1)}, f32[128,32,128]{0,2,1:T(8,128)}, u32[]{:S(2)}) copy-start(f32[128,32,128]{0,2,1:T(8,128)} %convolution_bitcast_fusion.1) | copy-start | bytes 6291460
where the time goes:
time: 610 us; the launch traced here: 603 us
  local copies, waits for them, and re-layouts  207 us (34%)
  waiting for transfers between devices  193 us (32%)
  other arithmetic  82 us (13%)
  starting transfers between devices  66.5 us (11%)
  matrix products  53.3 us (9%)
    all_to_all x1, waiting for transfers between devices, local(): lax.all_to_all(spectral, 'narrow', split_axis=2, concat_axis=3, tiled=True)  93.1 us
    scatter-add x1, other arithmetic, local(): jnp.zeros((size_x * size_y, depth), jnp.float32).at[targets]  59.9 us
    scatter x1, local copies, waits for them, and re-layouts, local(): weight_holder.at[wide_target, narrow_target, slot_position]  57.9 us
    all_to_all x1, waiting for transfers between devices, local(): lax.all_to_all(spectral, 'wide', split_axis=2, concat_axis=1, tiled=True)  44.2 us
    all_to_all x1, waiting for transfers between devices, local(): lax.all_to_all(spectral, 'narrow', split_axis=3, concat_axis=2, tiled=True)  30.5 us
    scatter x2, local copies, waits for them, and re-layouts, local(): assay_buf.at[wide_target, narrow_target, slot_position].set(assay[0])  30.3 us
    scatter x2, local copies, waits for them, and re-layouts, local(): index_buf.at[wide_target, narrow_target, slot_position].set(row_indices)  29.7 us
    dot_general x4, matrix products, transform(): jnp.einsum('sapqb,sptc->tacqb', four, dft_matrix(rows_p, sign), precision...  24.6 us
  transfers between devices with their start and end apart: 10, of which 5 were waited for; matrix products, arithmetic and copies ran while one was open for 39% of the time, Pallas kernels for 0%

commit v1 on v0

--- a/solution.py
+++ b/solution.py
@@ -9,6 +9,26 @@
 CELLS_THIRD = 128
 TARGET_PENCILS = 4
 highest = lax.Precision.HIGHEST
+
+
+def rest_series(incoming_x, bus_axis):
+    next_value = lax.axis_index(bus_axis)
+    b_next = lax.axis_size(bus_axis)
+    answer, piece_out = (b_next, next_value)
+    taken_in = list(incoming_x.shape)
+    near = incoming_x.shape[1] // answer
+    taken_in[1] = near
+    r1 = taken_in[1]
+    taken_in[1] = r1 * answer
+    block_next = jnp.zeros(taken_in, incoming_x.dtype)
+    for u in tuple(range(answer)):
+        passed = lax.dynamic_slice_in_dim(incoming_x, (piece_out ^ u) * near, near, axis=1)
+        if u:
+            passed = lax.ppermute(passed, bus_axis, [(c, c ^ u) for c in range(answer)])
+        block_next = lax.dynamic_update_slice_in_dim(
+            block_next, passed, (piece_out ^ u) * r1, axis=1
+        )
+    return block_next
 
 
 def pair_tables(cosine, sine):
@@ -119,12 +139,8 @@
     index_buf = jnp.zeros((n_wide, n_narrow, capacity, TARGET_PENCILS + 1), jnp.int32)
     index_buf = index_buf.at[wide_target, narrow_target, slot_position].set(row_indices)
     weight_got, assay_got, index_got = (
-        lax.all_to_all(
-            lax.all_to_all(weight_holder, "wide", split_axis=0, concat_axis=0, tiled=True),
-            "narrow",
-            split_axis=1,
-            concat_axis=1,
-            tiled=True,
+        rest_series(
+            lax.all_to_all(weight_holder, "wide", split_axis=0, concat_axis=0, tiled=True), "narrow"
         ),
         lax.all_to_all(
             lax.all_to_all(assay_buf, "wide", split_axis=0, concat_axis=0, tiled=True),

time: 610 us -> 589 us (0.966)
  waiting for transfers between devices: 193 us -> 163 us
  starting transfers between devices: 66.5 us -> 74.8 us
    all_to_all x1, waiting for transfers between devices: 30.5 us -> 90.9 us  [local(): lax.all_to_all(spectral, 'narrow', split_axis=3, concat_axis=2, tiled=True)]
    all_to_all x1, waiting for transfers between devices: 93.1 us -> 33.5 us  [local(): lax.all_to_all(spectral, 'narrow', split_axis=2, concat_axis=3, tiled=True)]
    all_to_all x1, waiting for transfers between devices: 44.2 us -> 0.01 us  [local(): lax.all_to_all(spectral, 'wide', split_axis=2, concat_axis=1, tiled=True)]
    ppermute x0 -> x7, waiting for transfers between devices: none -> 38.5 us  [rest_series(): passed = lax.ppermute(passed, bus_axis, [(c, c ^ u) for c in range(answer)])]
    all_to_all x1 -> x0, waiting for transfers between devices: 21.6 us -> none  [local(): lax.all_to_all(lax.all_to_all(weight_holder, 'wide', split_axis=0, concat...]
    ppermute x0 -> x7, starting transfers between devices: none -> 10.2 us  [rest_series(): passed = lax.ppermute(passed, bus_axis, [(c, c ^ u) for c in range(answer)])]
  transfers between devices with their start and end apart: 10 -> 16, of which waited for: 5 -> 8; matrix products, arithmetic and copies ran while one was open for 39% -> 41% of each run, Pallas kernels for 0% -> 0%
where the time goes in v1:
time: 589 us; the launch traced here: 581 us
  local copies, waits for them, and re-layouts  213 us (36%)
  waiting for transfers between devices  163 us (28%)
  other arithmetic  76.2 us (13%)
  starting transfers between devices  74.8 us (13%)
  matrix products  53.7 us (9%)
    all_to_all x1, waiting for transfers between devices, local(): lax.all_to_all(spectral, 'narrow', split_axis=3, concat_axis=2, tiled=True)  90.9 us
    scatter x1, local copies, waits for them, and re-layouts, local(): weight_holder.at[wide_target, narrow_target, slot_position]  60.1 us
    scatter-add x1, other arithmetic, local(): jnp.zeros((size_x * size_y, depth), jnp.float32).at[targets]  59.5 us
    ppermute x7, waiting for transfers between devices, rest_series(): passed = lax.ppermute(passed, bus_axis, [(c, c ^ u) for c in range(answer)])  38.5 us
    all_to_all x1, waiting for transfers between devices, local(): lax.all_to_all(spectral, 'narrow', split_axis=2, concat_axis=3, tiled=True)  33.5 us
    scatter x2, local copies, waits for them, and re-layouts, local(): assay_buf.at[wide_target, narrow_target, slot_position].set(assay[0])  30.3 us
    scatter x2, local copies, waits for them, and re-layouts, local(): index_buf.at[wide_target, narrow_target, slot_position].set(row_indices)  29.7 us
    dot_general x4, matrix products, transform(): jnp.einsum('sapqb,sptc->tacqb', four, dft_matrix(rows_p, sign), precision...  22.6 us
  transfers between devices with their start and end apart: 16, of which 8 were waited for; matrix products, arithmetic and copies ran while one was open for 41% of the time, Pallas kernels for 0%

profile of v1, /device:TPU:16, one launch (start us, length us, event | category | flops | bytes accessed | tf_op | source)
XLA Modules:
  0.0 581.3 jit_solution(13469354830271019915)
XLA Ops:
  1.6 6.0 %convolution_bitcast_fusion = f32[2,128,32,128]{3,1,2,0:T(8,128)S(1)} fusion(f32[128,32,128]{2,1,0:T(8,128)} %param.7, f32[1,128,128]{2,1,0:T(8,128)S(1)} %get-tuple-element.31, f32[1,128,128]{2,1,0:T(8,128)S(1)} %get-tuple-element.30), kind=kOutput, calls=%fused_computation.45 | convolution fusion | flops 1610645504 | bytes 6422528 | tf_op jit(solution)/shard_map/xyz,sqz->sqyx/dot_general | solution.py:101
  7.6 4.5 copy.218
  12.1 8.0 %all-to-all-start = ((f32[2,128,32,128]{3,2,0,1:T(8,128)}), f32[2,128,32,128]{3,2,0,1:T(8,128)}, u32[]{:S(2)}, u32[]{:S(2)}) async-start(f32[2,128,32,128]{3,2,0,1:T(8,128)} %copy.218), calls=%async_computation | async-start | bytes 8388608 | tf_op jit(solution)/shard_map/all_to_all | solution.py:103
  21.4 28.0 %scatter_fusion = s32[32,8,8,5]{3,2,1,0:T(8,128)S(1)} fusion(s32[32,8,8,5]{3,2,1,0:T(8,128)S(1)} %broadcast_in_dim.13, s32[512]{0:T(512)S(1)} %bitcast.211, s32[512,5]{1,0:T(8,128)S(1)} %copy.246), kind=kCustom, calls=%fused_computation.1 | custom fusion | bytes 36864 | tf_op jit(solution)/shard_map/scatter | solution.py:140
  52.1 29.6 %scatter_fusion.1 = bf16[32,8,8]{0,2,1:T(8,128)(2,1)S(1)} fusion(bf16[32,8,8]{0,2,1:T(8,128)(2,1)S(1)} %broadcast_in_dim.14, s32[512]{0:T(512)S(1)} %bitcast.212, bf16[512]{0:T(512)(128)(2,1)S(1)} %reduce), kind=kCustom, calls=%fused_computation.2 | custom fusion | bytes 9216 | tf_op jit(solution)/shard_map/scatter | solution.py:137
  83.3 7.3 %all-to-all-start.6 = ((bf16[32,8,8]{2,1,0:T(8,128)(2,1)}), bf16[32,8,8]{2,1,0:T(8,128)(2,1)S(1)}, u32[]{:S(2)}, u32[]{:S(2)}) async-start(bf16[32,8,8]{2,1,0:T(8,128)(2,1)} %copy.251), calls=%async_computation.6 | async-start | bytes 131072 | tf_op jit(solution)/shard_map/all_to_all | solution.py:146
  93.5 5.6 fusion.23
  101.9 7.8 %all-to-all-start.4 = ((s32[32,1,320]{2,1,0:T(1,128)}), s32[32,1,320]{2,1,0:T(1,128)S(1)}, u32[]{:S(2)}, u32[]{:S(2)}) async-start(s32[32,1,320]{2,1,0:T(1,128)} %reshape.696), calls=%async_computation.4 | async-start | bytes 98304 | tf_op jit(solution)/shard_map/all_to_all | solution.py:153
  109.7 6.6 %fusion.26 = f32[2,4,128,8,128]{4,2,3,1,0:T(8,128)S(1)} fusion(f32[2,4,8,128,128]{4,2,3,1,0:T(8,128)} %pad_maximum_fusion, f32[1,128,2,128]{1,3,0,2:T(8,128)S(1)} %get-tuple-element.22, f32[1,128,2,128]{1,3,0,2:T(8,128)S(1)} %get-tuple-element.23), kind=kOutput, calls=%fused_computation.38 | convolution fusion | flops 3221291008 | bytes 8650752 | tf_op jit(solution)/shard_map/sacqb,sqtd->tadcb/dot_general | solution.py:81
  118.7 4.7 copy.226
  123.4 8.5 %all-to-all-start.1 = ((f32[2,4,128,1024]{2,1,0,3:T(4,128)}), f32[2,4,128,1024]{2,1,0,3:T(4,128)}, u32[]{:S(2)}, u32[]{:S(2)}) async-start(f32[2,4,128,1024]{2,1,0,3:T(4,128)} %copy.226), calls=%async_computation.1 | async-start | bytes 8388608 | tf_op jit(solution)/shard_map/all_to_all | solution.py:106
  137.8 90.9 %all-to-all-done.1 = f32[2,4,128,1024]{2,1,0,3:T(4,128)} async-done(((f32[2,4,128,1024]{2,1,0,3:T(4,128)}), f32[2,4,128,1024]{2,1,0,3:T(4,128)}, u32[]{:S(2)}, u32[]{:S(2)}) %all-to-all-start.1) | async-done | bytes 4194336 | tf_op jit(solution)/shard_map/all_to_all | solution.py:106
  236.1 5.6 fusion.44
  249.9 6.0 %fusion.32 = f32[2,4,8,128,128]{4,2,3,1,0:T(8,128)S(1)} fusion(f32[2,4,8,128,128]{4,3,2,1,0:T(8,128)S(1)} %bitcast_multiply_fusion, f32[1,8,2,8]{1,3,0,2:T(8,128)S(1)} %copy.213, f32[1,8,2,8]{1,3,0,2:T(8,128)S(1)} %copy.212), kind=kOutput, calls=%fused_computation.40 | convolution fusion | flops 201326848 | bytes 8389632 | tf_op jit(solution)/shard_map/sapqb,sptc->tacqb/dot_general | solution.py:70
  258.8 7.1 %all-to-all-start.5 = ((s32[8,1,1280]{2,1,0:T(1,128)}), s32[8,1,1280]{2,1,0:T(1,128)S(1)}, u32[]{:S(2)}, u32[]{:S(2)}) async-start(s32[8,1,1280]{2,1,0:T(1,128)} %reshape.698), calls=%async_computation.5 | async-start | bytes 81920 | tf_op jit(solution)/shard_map/all_to_all | solution.py:152
  265.9 6.6 %fusion.35 = f32[2,4,128,8,128]{4,2,3,1,0:T(8,128)S(1)} fusion(f32[2,4,8,128,128]{4,2,3,1,0:T(8,128)} %pad_maximum_fusion.2, f32[1,128,2,128]{1,3,2,0:T(8,128)S(1)} %get-tuple-element.24, f32[1,128,2,128]{1,3,2,0:T(8,128)S(1)} %get-tuple-element.21), kind=kOutput, calls=%fused_computation.41 | convolution fusion | flops 3221291008 | bytes 8650752 | tf_op jit(solution)/shard_map/sacqb,sqtd->tadcb/dot_general | solution.py:81
  274.8 4.7 copy.235
  279.6 7.4 %all-to-all-start.2 = ((f32[2,4,1024,128]{3,1,0,2:T(4,128)}), f32[2,4,1024,128]{3,1,0,2:T(4,128)}, u32[]{:S(2)}, u32[]{:S(2)}) async-start(f32[2,4,1024,128]{3,1,0,2:T(4,128)} %copy.235), calls=%async_computation.2 | async-start | bytes 8388608 | tf_op jit(solution)/shard_map/all_to_all | solution.py:111
  289.3 60.1 %scatter_fusion.2 = bf16[32,8,8,4,128]{4,3,2,1,0:T(4,128)(2,1)} fusion(bf16[32,8,8,4,128]{4,3,2,1,0:T(4,128)(2,1)} %broadcast.896.clone, s32[512]{0:T(512)S(1)} %bitcast.213, bf16[512,4,128]{2,1,0:T(4,128)(2,1)S(1)} %bitcast.229), kind=kCustom, calls=%fused_computation.3 | custom fusion | bytes 1579008 | tf_op jit(solution)/shard_map/scatter | solution.py:133
  349.4 33.5 %all-to-all-done.2 = f32[2,4,1024,128]{3,1,0,2:T(4,128)} async-done(((f32[2,4,1024,128]{3,1,0,2:T(4,128)}), f32[2,4,1024,128]{3,1,0,2:T(4,128)}, u32[]{:S(2)}, u32[]{:S(2)}) %all-to-all-start.2) | async-done | bytes 4194336 | tf_op jit(solution)/shard_map/all_to_all | solution.py:111
  382.8 7.4 %all-to-all-start.8 = ((bf16[32,8,8,4,128]{4,3,2,1,0:T(4,128)(2,1)}), bf16[32,8,8,4,128]{4,3,2,1,0:T(4,128)(2,1)S(1)}, u32[]{:S(2)}, u32[]{:S(2)}) async-start(bf16[32,8,8,4,128]{4,3,2,1,0:T(4,128)(2,1)} %scatter_fusion.2), calls=%async_computation.8 | async-start | bytes 4194304 | tf_op jit(solution)/shard_map/all_to_all | solution.py:143
  390.2 5.0 copy.236
  395.2 5.4 copy.238
  400.7 5.4 fusion.38
  413.5 4.7 copy.242
  418.2 7.8 %all-to-all-start.3 = ((f32[2,4,1024,128]{3,1,0,2:T(4,128)}), f32[2,4,1024,128]{3,1,0,2:T(4,128)}, u32[]{:S(2)}, u32[]{:S(2)}) async-start(f32[2,4,1024,128]{3,1,0,2:T(4,128)} %copy.242), calls=%async_computation.3 | async-start | bytes 8388608 | tf_op jit(solution)/shard_map/all_to_all | solution.py:117
  441.3 5.1 collective-permute-done
  447.2 15.6 %collective-permute-done.1 = bf16[32,1,8,4,128]{4,3,2,1,0:T(4,128)(2,1)S(1)} collective-permute-done((bf16[32,1,8,4,128]{4,3,2,1,0:T(4,128)(2,1)S(1)}, bf16[32,1,8,4,128]{4,3,2,1,0:T(4,128)(2,1)S(1)}, u32[]{:S(2)}, u32[]{:S(2)}) %collective-permute-start.1) | collective-permute-done | bytes 262176 | tf_op jit(solution)/shard_map/ppermute | solution.py:27
  465.5 7.4 %collective-permute-done.2 = bf16[32,1,8,4,128]{4,3,2,1,0:T(4,128)(2,1)S(1)} collective-permute-done((bf16[32,1,8,4,128]{4,3,2,1,0:T(4,128)(2,1)S(1)}, bf16[32,1,8,4,128]{4,3,2,1,0:T(4,128)(2,1)S(1)}, u32[]{:S(2)}, u32[]{:S(2)}) %collective-permute-start.2) | collective-permute-done | bytes 262176 | tf_op jit(solution)/shard_map/ppermute | solution.py:27
  473.8 4.5 collective-permute-done.3
  499.3 11.8 %gather_fusion = f32[2048]{0:T(1024)S(1)} fusion(f32[524288]{0:T(1024)S(1)} %bitcast.214, s32[2048]{0:T(1024)S(1)} %broadcast_clamp_fusion), kind=kCustom, calls=%fused_computation | custom fusion | bytes 24576 | tf_op jit(solution)/shard_map/gather | solution.py:163
  512.1 59.5 %scatter_custom_fusion.3 = f32[4096,128]{1,0:T(8,128)} fusion(s32[8192]{0:T(1024)S(1)} %bitcast.232, bf16[8192,128]{1,0:T(8,128)(2,1)} %bitcast.109, f32[8192]{0:T(1024)S(1)} %mul.834, f32[]{:T(128)} %constant.186.clone.1), kind=kCustom, calls=%fused_computation.10 | custom fusion | flops 3145728 | bytes 4227076 | tf_op jit(solution)/shard_map/scatter-add | solution.py:169
  (129 shorter events, 102.1 us)
Async XLA Ops:
  1.0 0.6 copy-start.1
  12.1 8.7 %copy-start.9 = (s32[1,512,4]{1,2,0:T(4,128)S(1)}, s32[1,512,4]{1,2,0:T(4,128)}, u32[]{:S(2)}) copy-start(s32[1,512,4]{1,2,0:T(4,128)} %param.13) | copy-start | bytes 24580
  12.1 8.7 %copy-start.11 = (s32[1,512]{1,0:T(1,128)S(1)}, s32[1,512]{1,0:T(1,128)}, u32[]{:S(2)}) copy-start(s32[1,512]{1,0:T(1,128)} %param.12) | copy-start | bytes 6148
  12.1 8.9 %copy-start.8 = (s32[1,512]{1,0:T(1,128)S(1)}, s32[1,512]{1,0:T(1,128)}, u32[]{:S(2)}) copy-start(s32[1,512]{1,0:T(1,128)} %param.11) | copy-start | bytes 6148
  12.1 71.2 %all-to-all-start = ((f32[2,128,32,128]{3,2,0,1:T(8,128)}), f32[2,128,32,128]{3,2,0,1:T(8,128)}, u32[]{:S(2)}, u32[]{:S(2)}) async-start(f32[2,128,32,128]{3,2,0,1:T(8,128)} %copy.218), calls=%async_computation | async-start | bytes 8388608 | tf_op jit(solution)/shard_map/all_to_all | solution.py:103
  20.8 78.3 %copy-start.3 = (f32[8,128]{0,1:T(8,128)}, f32[8,128]{0,1:T(8,128)S(1)}, u32[]{:S(2)}) copy-start(f32[8,128]{0,1:T(8,128)S(1)} %copy.223) | copy-start | bytes 12292
  49.3 2.8 copy-start.10
  83.3 18.6 %all-to-all-start.6 = ((bf16[32,8,8]{2,1,0:T(8,128)(2,1)}), bf16[32,8,8]{2,1,0:T(8,128)(2,1)S(1)}, u32[]{:S(2)}, u32[]{:S(2)}) async-start(bf16[32,8,8]{2,1,0:T(8,128)(2,1)} %copy.251), calls=%async_computation.6 | async-start | bytes 131072 | tf_op jit(solution)/shard_map/all_to_all | solution.py:146
  101.9 21.5 %all-to-all-start.4 = ((s32[32,1,320]{2,1,0:T(1,128)}), s32[32,1,320]{2,1,0:T(1,128)S(1)}, u32[]{:S(2)}, u32[]{:S(2)}) async-start(s32[32,1,320]{2,1,0:T(1,128)} %reshape.696), calls=%async_computation.4 | async-start | bytes 98304 | tf_op jit(solution)/shard_map/all_to_all | solution.py:153
  123.4 105.3 %all-to-all-start.1 = ((f32[2,4,128,1024]{2,1,0,3:T(4,128)}), f32[2,4,128,1024]{2,1,0,3:T(4,128)}, u32[]{:S(2)}, u32[]{:S(2)}) async-start(f32[2,4,128,1024]{2,1,0,3:T(4,128)} %copy.226), calls=%async_computation.1 | async-start | bytes 8388608 | tf_op jit(solution)/shard_map/all_to_all | solution.py:106
  228.7 30.1 %all-to-all-start.7 = ((bf16[8,2,128]{2,1,0:T(2,128)(2,1)}), bf16[8,2,128]{2,1,0:T(2,128)(2,1)S(1)}, u32[]{:S(2)}, u32[]{:S(2)}) async-start(bf16[8,2,128]{2,1,0:T(2,128)(2,1)} %reshape.694), calls=%async_computation.7 | async-start | bytes 8192 | tf_op jit(solution)/shard_map/all_to_all | solution.py:145
  236.1 5.6 copy-start.4
  249.9 6.0 %copy-start.5 = (f32[8,128]{0,1:T(8,128)S(1)}, f32[8,128]{0,1:T(8,128)}, u32[]{:S(2)}) copy-start(f32[8,128]{0,1:T(8,128)} %copy.231) | copy-start | bytes 12292
  258.8 20.8 %all-to-all-start.5 = ((s32[8,1,1280]{2,1,0:T(1,128)}), s32[8,1,1280]{2,1,0:T(1,128)S(1)}, u32[]{:S(2)}, u32[]{:S(2)}) async-start(s32[8,1,1280]{2,1,0:T(1,128)} %reshape.698), calls=%async_computation.5 | async-start | bytes 81920 | tf_op jit(solution)/shard_map/all_to_all | solution.py:152
  279.6 103.3 %all-to-all-start.2 = ((f32[2,4,1024,128]{3,1,0,2:T(4,128)}), f32[2,4,1024,128]{3,1,0,2:T(4,128)}, u32[]{:S(2)}, u32[]{:S(2)}) async-start(f32[2,4,1024,128]{3,1,0,2:T(4,128)} %copy.235), calls=%async_computation.2 | async-start | bytes 8388608 | tf_op jit(solution)/shard_map/all_to_all | solution.py:111
  287.0 2.3 copy-start.6
  382.8 35.4 %all-to-all-start.8 = ((bf16[32,8,8,4,128]{4,3,2,1,0:T(4,128)(2,1)}), bf16[32,8,8,4,128]{4,3,2,1,0:T(4,128)(2,1)S(1)}, u32[]{:S(2)}, u32[]{:S(2)}) async-start(bf16[32,8,8,4,128]{4,3,2,1,0:T(4,128)(2,1)} %scatter_fusion.2), calls=%async_computation.8 | async-start | bytes 4194304 | tf_op jit(solution)/shard_map/all_to_all | solution.py:143
  418.2 69.3 %all-to-all-start.3 = ((f32[2,4,1024,128]{3,1,0,2:T(4,128)}), f32[2,4,1024,128]{3,1,0,2:T(4,128)}, u32[]{:S(2)}, u32[]{:S(2)}) async-start(f32[2,4,1024,128]{3,1,0,2:T(4,128)} %copy.242), calls=%async_computation.3 | async-start | bytes 8388608 | tf_op jit(solution)/shard_map/all_to_all | solution.py:117
  433.0 13.4 %collective-permute-start = (bf16[32,1,8,4,128]{4,3,2,1,0:T(4,128)(2,1)S(1)}, bf16[32,1,8,4,128]{4,3,2,1,0:T(4,128)(2,1)S(1)}, u32[]{:S(2)}, u32[]{:S(2)}) collective-permute-start(bf16[32,1,8,4,128]{4,3,2,1,0:T(4,128)(2,1)S(1)} %get-tuple-element.19), channel_id=1, source_target_pairs={{0,1},{1,0},{2,3},{3,2},{4,5},{5,4},{6,7},{7,6},{8,9},{9,8},{10,11... | collective-permute-start | bytes 786440 | tf_op jit(solution)/shard_map/ppermute | solution.py:27
  433.3 29.5 %collective-permute-start.1 = (bf16[32,1,8,4,128]{4,3,2,1,0:T(4,128)(2,1)S(1)}, bf16[32,1,8,4,128]{4,3,2,1,0:T(4,128)(2,1)S(1)}, u32[]{:S(2)}, u32[]{:S(2)}) collective-permute-start(bf16[32,1,8,4,128]{4,3,2,1,0:T(4,128)(2,1)S(1)} %get-tuple-element.18), channel_id=1, source_target_pairs={{0,2},{1,3},{2,0},{3,1},{4,6},{5,7},{6,4},{7,5},{8,10},{9,11},{10,... | collective-permute-start | bytes 786440 | tf_op jit(solution)/shard_map/ppermute | solution.py:27
  433.4 39.6 %collective-permute-start.2 = (bf16[32,1,8,4,128]{4,3,2,1,0:T(4,128)(2,1)S(1)}, bf16[32,1,8,4,128]{4,3,2,1,0:T(4,128)(2,1)S(1)}, u32[]{:S(2)}, u32[]{:S(2)}) collective-permute-start(bf16[32,1,8,4,128]{4,3,2,1,0:T(4,128)(2,1)S(1)} %get-tuple-element.17), channel_id=1, source_target_pairs={{0,3},{1,2},{2,1},{3,0},{4,7},{5,6},{6,5},{7,4},{8,11},{9,10},{10,... | collective-permute-start | bytes 786440 | tf_op jit(solution)/shard_map/ppermute | solution.py:27
  437.5 40.7 %collective-permute-start.3 = (bf16[32,1,8,4,128]{4,3,2,1,0:T(4,128)(2,1)S(1)}, bf16[32,1,8,4,128]{4,3,2,1,0:T(4,128)(2,1)S(1)}, u32[]{:S(2)}, u32[]{:S(2)}) collective-permute-start(bf16[32,1,8,4,128]{4,3,2,1,0:T(4,128)(2,1)S(1)} %get-tuple-element.16), channel_id=1, source_target_pairs={{0,4},{1,5},{2,6},{3,7},{4,0},{5,1},{6,2},{7,3},{8,12},{9,13},{10,... | collective-permute-start | bytes 786440 | tf_op jit(solution)/shard_map/ppermute | solution.py:27
  437.8 44.1 %collective-permute-start.4 = (bf16[32,1,8,4,128]{4,3,2,1,0:T(4,128)(2,1)S(1)}, bf16[32,1,8,4,128]{4,3,2,1,0:T(4,128)(2,1)S(1)}, u32[]{:S(2)}, u32[]{:S(2)}) collective-permute-start(bf16[32,1,8,4,128]{4,3,2,1,0:T(4,128)(2,1)S(1)} %get-tuple-element.15), channel_id=1, source_target_pairs={{0,5},{1,4},{2,7},{3,6},{4,1},{5,0},{6,3},{7,2},{8,13},{9,12},{10,... | collective-permute-start | bytes 786440 | tf_op jit(solution)/shard_map/ppermute | solution.py:27
  446.4 36.3 %collective-permute-start.5 = (bf16[32,1,8,4,128]{4,3,2,1,0:T(4,128)(2,1)S(1)}, bf16[32,1,8,4,128]{4,3,2,1,0:T(4,128)(2,1)S(1)}, u32[]{:S(2)}, u32[]{:S(2)}) collective-permute-start(bf16[32,1,8,4,128]{4,3,2,1,0:T(4,128)(2,1)S(1)} %get-tuple-element.14), channel_id=1, source_target_pairs={{0,6},{1,7},{2,4},{3,5},{4,2},{5,3},{6,0},{7,1},{8,14},{9,15},{10,... | collective-permute-start | bytes 786440 | tf_op jit(solution)/shard_map/ppermute | solution.py:27
  462.8 23.9 %collective-permute-start.6 = (bf16[32,1,8,4,128]{4,3,2,1,0:T(4,128)(2,1)S(1)}, bf16[32,1,8,4,128]{4,3,2,1,0:T(4,128)(2,1)S(1)}, u32[]{:S(2)}, u32[]{:S(2)}) collective-permute-start(bf16[32,1,8,4,128]{4,3,2,1,0:T(4,128)(2,1)S(1)} %get-tuple-element.13), channel_id=1, source_target_pairs={{0,7},{1,6},{2,5},{3,4},{4,3},{5,2},{6,1},{7,0},{8,15},{9,14},{10,... | collective-permute-start | bytes 786440 | tf_op jit(solution)/shard_map/ppermute | solution.py:27
  490.5 2.7 copy-start.2
  490.6 2.7 copy-start.7
  571.5 3.1 copy-start
